TPU v7x, 256 devices: a whole 4x4x8 slice. The times are simulated.
256 devices in a mesh: row: 8 (over y, core), col: 32 (over x, z).
Axes of the slice: x: 4, y: 4, z: 8, core: 2. Of those that a mesh axis runs over, the one named last changes fastest.
Arguments:
- tokens: bfloat16 [512, 8192], P('col', 'row'), may hold values from -6 to 6
- out_grad: bfloat16 [512, 8192], P('col', 'row'), may hold values from -6 to 6
- gate_weight: bfloat16 [8192, 28672], P('row', 'col'), may hold values from -0.0625 to 0.0625
- up_weight: bfloat16 [8192, 28672], P('row', 'col'), may hold values from -0.0625 to 0.0625
- down_weight: bfloat16 [28672, 8192], P('col', 'row'), may hold values from -0.03125 to 0.03125
Outputs:
- input_grad: bfloat16 [512, 8192], P('col', 'row')
- gate_grad: bfloat16 [8192, 28672], P('row', 'col')
- up_grad: bfloat16 [8192, 28672], P('row', 'col')
- down_grad: bfloat16 [28672, 8192], P('col', 'row')
All inputs are finite; a program needn't handle non-finite values.
Results may differ from a plain program's by a relative error of at most 0.005.
Values may be sent and summed in bfloat16 or wider, within the bound.
No kernel may reach another device: no remote copies, remote signals or barrier semaphores. Data moves between devices by JAX's collectives and lax.ppermute only.
A program may use at most 64 MiB of HBM per device.

v0:
```python
import jax
import jax.numpy as jnp
from jax import lax
from jax.sharding import PartitionSpec as P


def contract_first(left, right):
    return lax.dot_general(
        left, right, (((0,), (0,)), ((), ())), preferred_element_type=jnp.float32
    )


def contract_last(left, right):
    return lax.dot_general(
        left, right, (((1,), (1,)), ((), ())), preferred_element_type=jnp.float32
    )


def local_deltas(sums, width):
    gate = sums[:, :width]
    up = sums[:, width : 2 * width]
    hidden_grad = sums[:, 2 * width :]
    sig = jax.nn.sigmoid(gate)
    act = gate * sig
    hidden = (act * up).astype(jnp.bfloat16)
    gate_delta = (hidden_grad * up * sig * (1.0 + gate * (1.0 - sig))).astype(jnp.bfloat16)
    up_delta = (hidden_grad * act).astype(jnp.bfloat16)
    return (hidden, gate_delta, up_delta)


def per_device(tokens, out_grad, gate_weight, up_weight, down_weight):
    width = gate_weight.shape[1]
    token_panel, grad_panel = (
        lax.all_gather(tokens, "col", axis=0, tiled=True),
        lax.all_gather(out_grad, "col", axis=0, tiled=True),
    )
    gate_part = jnp.dot(token_panel, gate_weight, preferred_element_type=jnp.float32)
    up_part = jnp.dot(token_panel, up_weight, preferred_element_type=jnp.float32)
    back_part = contract_last(grad_panel, down_weight)
    sums = lax.psum_scatter(
        jnp.concatenate([gate_part, up_part, back_part], axis=1),
        "row",
        scatter_dimension=0,
        tiled=True,
    )
    hidden_share, gate_share, up_share = local_deltas(sums, width)
    hidden, gate_delta, up_delta = (
        lax.all_gather(hidden_share, "row", axis=0, tiled=True),
        lax.all_gather(gate_share, "row", axis=0, tiled=True),
        lax.all_gather(up_share, "row", axis=0, tiled=True),
    )
    down_grad = contract_first(hidden, grad_panel).astype(jnp.bfloat16)
    gate_grad = contract_first(token_panel, gate_delta).astype(jnp.bfloat16)
    up_grad = contract_first(token_panel, up_delta).astype(jnp.bfloat16)
    input_grad = lax.psum_scatter(
        contract_last(gate_delta, gate_weight) + contract_last(up_delta, up_weight),
        "col",
        scatter_dimension=0,
        tiled=True,
    ).astype(jnp.bfloat16)
    return (input_grad, gate_grad, up_grad, down_grad)


def solution(mesh):
    return jax.shard_map(
        per_device,
        mesh=mesh,
        in_specs=(
            P("col", "row"),
            P("col", "row"),
            P("row", "col"),
            P("row", "col"),
            P("col", "row"),
        ),
        out_specs=(P("col", "row"), P("row", "col"), P("row", "col"), P("col", "row")),
        check_vma=False,
    )
```

profile of v0, /device:TPU:8, one launch (start us, length us, event | category | flops | bytes accessed | tf_op | source)
XLA Modules:
  0.0 470.2 jit_solution(882471276423203136)
XLA Ops:
  7.2 0.7 all-gather.3.cloned.1.call-update
  8.0 0.7 all-gather.5.cloned.1.call-update
  8.7 80.9 %all-gather.3.cloned.1.call-done = bf16[512,1024]{1,0:T(8,128)(2,1)} async-done(((bf16[16,1024]{1,0:T(8,128)(2,1)}), bf16[512,1024]{1,0:T(8,128)(2,1)}) %all-gather.3.cloned.1.call-update) | async-done | bytes 1048592 | tf_op jit(solution)/shard_map/all_gather | solution.py:34
  89.6 4.4 fusion.2
  94.0 2.5 fusion.1
  96.5 69.5 %all-gather.5.cloned.1.call-done = bf16[512,1024]{1,0:T(8,128)(2,1)} async-done(((bf16[16,1024]{1,0:T(8,128)(2,1)}), bf16[512,1024]{1,0:T(8,128)(2,1)}) %all-gather.5.cloned.1.call-update) | async-done | bytes 1048592 | tf_op jit(solution)/shard_map/all_gather | solution.py:35
  166.0 3.2 fusion.3
  169.2 2.8 pad_maximum_fusion
  172.0 0.0 reduce-scatter.5.cloned.1.call-start
  172.1 37.5 %reduce-scatter.3.cloned.1.call-done = f32[64,2688]{1,0:T(8,128)} async-done(((f32[512,2688]{1,0:T(8,128)}), f32[64,2688]{1,0:T(8,128)}) %reduce-scatter.3.cloned.1.call-update) | async-done | bytes 688144 | tf_op jit(solution)/shard_map/reduce_scatter | solution.py:40
  209.6 1.3 multiply_convert_fusion
  210.9 15.0 %all_gather.17 = bf16[512,896]{1,0:T(8,128)(2,1)S(1)} all-gather(bf16[64,896]{1,0:T(8,128)(2,1)S(1)} %get-tuple-element.9), channel_id=1, replica_groups=mesh['row'=8,'col'=32] {'row'}, dimensions={0}, use_global_device_ids=true | all-gather | bytes 1032192 | tf_op jit(solution)/shard_map/all_gather | solution.py:49
  226.0 13.5 %all_gather.18 = bf16[512,896]{1,0:T(8,128)(2,1)S(1)} all-gather(bf16[64,896]{1,0:T(8,128)(2,1)S(1)} %get-tuple-element.10), channel_id=1, replica_groups=mesh['row'=8,'col'=32] {'row'}, dimensions={0}, use_global_device_ids=true | all-gather | bytes 1032192 | tf_op jit(solution)/shard_map/all_gather | solution.py:50
  239.5 1.3 fusion.4
  240.8 0.5 copy-done.4
  241.3 2.6 convolution_add_fusion
  243.9 3.9 convert_bitcast_fusion
  247.8 3.8 copy.10
  251.6 3.6 convert_bitcast_fusion.1
  255.2 3.8 copy.9
  259.0 13.5 %all_gather.19 = bf16[512,896]{1,0:T(8,128)(2,1)S(1)} all-gather(bf16[64,896]{1,0:T(8,128)(2,1)S(1)} %get-tuple-element.8), channel_id=1, replica_groups=mesh['row'=8,'col'=32] {'row'}, dimensions={0}, use_global_device_ids=true | all-gather | bytes 1032192 | tf_op jit(solution)/shard_map/all_gather | solution.py:48
  272.5 3.6 convolution_convert_fusion
  276.1 186.1 %reduce-scatter.5.cloned.1.call-done = f32[16,1024]{1,0:T(8,128)} async-done(((f32[512,1024]{1,0:T(8,128)}), f32[16,1024]{1,0:T(8,128)}) %reduce-scatter.5.cloned.1.call-update) | async-done | bytes 65552 | tf_op jit(solution)/shard_map/reduce_scatter | solution.py:55
  462.2 1.5 convert_element_type.29
  (16 shorter events, 0.2 us)
Async XLA Ops:
  7.2 86.8 %copy-start = (bf16[1024,896]{1,0:T(8,128)(2,1)S(1)}, bf16[1024,896]{1,0:T(8,128)(2,1)}, u32[]{:S(2)}) copy-start(bf16[1024,896]{1,0:T(8,128)(2,1)} %param.7) | copy-start | bytes 5505028
  7.2 82.4 %all-gather.3.cloned.1.call-start = ((), (), s32[]{:S(2)}) async-start(), calls=%async_computation.2 | async-start | bytes 1081344 | tf_op jit(solution)/shard_map/all_gather | solution.py:34
  7.9 158.1 %all-gather.5.cloned.1.call-start = ((), (), s32[]{:S(2)}) async-start(), calls=%async_computation.3 | async-start | bytes 1081344 | tf_op jit(solution)/shard_map/all_gather | solution.py:35
  8.7 201.0 %reduce-scatter.3.cloned.1.call-start = ((), (), s32[]{:S(2)}) async-start(), calls=%async_computation.4 | async-start | bytes 6193152 | tf_op jit(solution)/shard_map/reduce_scatter | solution.py:40
  89.6 4.4 copy-start.5
  166.0 3.3 copy-start.1
  166.0 3.3 copy-start.2
  172.0 290.2 %reduce-scatter.5.cloned.1.call-start = ((), (), s32[]{:S(2)}) async-start(), calls=%async_computation.5 | async-start | bytes 2162688 | tf_op jit(solution)/shard_map/reduce_scatter | solution.py:55
  239.5 1.3 copy-start.3
  239.5 1.8 copy-start.4
Sparse Core Ops, SparseCore 0:
  10.6 78.9 all-gather.2
  92.2 73.7 all-gather.4
  172.2 37.4 reduce-scatter.2
  244.0 218.1 reduce-scatter.4
where the time goes:
time: 471 us; the launch traced here: 470 us
  waiting for transfers between devices  375 us (80%)
  blocking collectives  42 us (9%)
  matrix products  25.1 us (5%)
  between operations  13.8 us (3%)
  local copies, waits for them, and re-layouts  8.16 us (2%)
  other arithmetic  5.51 us (1%)
    reduce_scatter x1, waiting for transfers between devices, per_device(): lax.psum_scatter(contract_last(gate_delta, gate_weight) + contract_last(u...  186 us
    all_gather x1, waiting for transfers between devices, per_device(): lax.all_gather(tokens, 'col', axis=0, tiled=True)  80.9 us
    all_gather x1, waiting for transfers between devices, per_device(): lax.all_gather(out_grad, 'col', axis=0, tiled=True)  69.5 us
    reduce_scatter x1, waiting for transfers between devices, per_device(): lax.psum_scatter(jnp.concatenate([gate_part, up_part, back_part], axis=1)...  37.5 us
    all_gather x1, blocking collectives, per_device(): lax.all_gather(gate_share, 'row', axis=0, tiled=True)  15 us
    all_gather x1, blocking collectives, per_device(): lax.all_gather(hidden_share, 'row', axis=0, tiled=True)  13.5 us
    all_gather x1, blocking collectives, per_device(): lax.all_gather(up_share, 'row', axis=0, tiled=True)  13.5 us
    dot_general x3, matrix products, contract_first(): lax.dot_general(left, right, (((0,), (0,)), ((), ())), preferred_element_...  11.1 us
  transfers between devices with their start and end apart: 4, of which 4 were waited for; matrix products, arithmetic and copies ran while one was open for 5% of the time, Pallas kernels for 0%

commit v1 on v0

v1 whole, which is shorter than its diff:
```python
import jax
import jax.numpy as jnp
from jax import lax
from jax.sharding import PartitionSpec as P

BF16, F32 = jnp.bfloat16, jnp.float32
NX, NZ, NY = 4, 8, 4
Z_GROUPS = [[x * NZ + z for z in range(NZ)] for x in range(NX)]


def x_shift(k):
    return [(x * NZ + z, (x + k) % NX * NZ + z) for x in range(NX) for z in range(NZ)]


def y_shift(k):
    return [(y * 2 + c, (y + k) % NY * 2 + c) for y in range(NY) for c in range(2)]


CORE_SWAP = [(y * 2 + c, y * 2 + 1 - c) for y in range(NY) for c in range(2)]


def contract_first(left, right):
    return lax.dot_general(left, right, (((0,), (0,)), ((), ())), preferred_element_type=F32)


def contract_last(left, right):
    return lax.dot_general(left, right, (((1,), (1,)), ((), ())), preferred_element_type=F32)


def gather_z(block):
    copies = jnp.broadcast_to(block[None], (NZ,) + block.shape)
    got = lax.all_to_all(copies, "col", 0, 0, axis_index_groups=Z_GROUPS, tiled=True)
    return got.reshape(NZ * block.shape[0], block.shape[1])


def gather_x(plane):
    parts = [plane] + [lax.ppermute(plane, "col", x_shift(k)) for k in (1, 3, 2)]
    return jnp.concatenate(parts, axis=0)


def per_device(tokens, out_grad, gate_weight, up_weight, down_weight):
    width = gate_weight.shape[1]
    row = lax.axis_index("row")
    y, core = row // 2, row % 2
    token_panel = gather_x(gather_z(tokens))
    grad_panel = gather_x(gather_z(out_grad))
    count = token_panel.shape[0]
    half, quarter = count // 2, count // 8

    gate_part = jnp.dot(token_panel, gate_weight, preferred_element_type=F32)
    up_part = jnp.dot(token_panel, up_weight, preferred_element_type=F32)
    back_part = contract_last(grad_panel, down_weight)

    def sum_over_row(part):
        mine = lax.dynamic_slice_in_dim(part, core * half, half, 0)
        other = lax.dynamic_slice_in_dim(part, (1 - core) * half, half, 0)
        pair = mine + lax.ppermute(other, "row", CORE_SWAP)
        total = lax.dynamic_slice_in_dim(pair, y * quarter, quarter, 0)
        for k in (2, 1, 3):
            piece = lax.dynamic_slice_in_dim(pair, (y + k) % NY * quarter, quarter, 0)
            total = total + lax.ppermute(piece.astype(BF16), "row", y_shift(k)).astype(F32)
        return total

    gate, up, hidden_grad = (sum_over_row(part) for part in (gate_part, up_part, back_part))
    sig = jax.nn.sigmoid(gate)
    act = gate * sig
    hidden = (act * up).astype(BF16)
    gate_delta = (hidden_grad * up * sig * (1.0 + gate * (1.0 - sig))).astype(BF16)
    up_delta = (hidden_grad * act).astype(BF16)

    def gather_over_row(share):
        mine = jnp.zeros((half, share.shape[1]), BF16)
        mine = lax.dynamic_update_slice_in_dim(mine, share, y * quarter, 0)
        for k in (2, 1, 3):
            got = lax.ppermute(share, "row", y_shift(k))
            mine = lax.dynamic_update_slice_in_dim(mine, got, (y - k) % NY * quarter, 0)
        other = lax.ppermute(mine, "row", CORE_SWAP)
        return jnp.where(
            core == 0, jnp.concatenate([mine, other], 0), jnp.concatenate([other, mine], 0)
        )

    deltas = gather_over_row(jnp.concatenate([gate_delta, up_delta], axis=1))
    hidden = gather_over_row(hidden)
    gate_delta, up_delta = deltas[:, :width], deltas[:, width:]

    partial = contract_last(gate_delta, gate_weight) + contract_last(up_delta, up_weight)
    planes = partial.reshape(NX, count // NX, partial.shape[1])
    plane_sum = planes[0]
    for at, k in ((3, 2), (1, 3), (2, 1)):
        plane_sum = plane_sum + lax.ppermute(planes[at].astype(BF16), "col", x_shift(k)).astype(F32)
    pieces = plane_sum.reshape(NZ, count // (NX * NZ), partial.shape[1]).astype(BF16)
    pieces = lax.all_to_all(pieces, "col", 0, 0, axis_index_groups=Z_GROUPS, tiled=True)
    input_grad = jnp.sum(pieces.astype(F32), axis=0).astype(BF16)

    down_grad = contract_first(hidden, grad_panel).astype(BF16)
    gate_grad = contract_first(token_panel, gate_delta).astype(BF16)
    up_grad = contract_first(token_panel, up_delta).astype(BF16)
    return (input_grad, gate_grad, up_grad, down_grad)


def solution(mesh):
    return jax.shard_map(
        per_device,
        mesh=mesh,
        in_specs=(
            P("col", "row"),
            P("col", "row"),
            P("row", "col"),
            P("row", "col"),
            P("col", "row"),
        ),
        out_specs=(P("col", "row"), P("row", "col"), P("row", "col"), P("col", "row")),
        check_vma=False,
    )
```

time: 471 us -> 146 us (0.31)
  waiting for transfers between devices: 375 us -> 36.9 us
  starting transfers between devices: 0.16 us -> 51.6 us
  blocking collectives: 42 us -> 20.1 us
  between operations: 13.8 us -> 1.06 us
  matrix products: 25.1 us -> 16.7 us
    reduce_scatter x2 -> x0, waiting for transfers between devices: 224 us -> none  [the longest x1 186 us: per_device(): lax.psum_scatter(contract_last(gate_delta, gate_weight) + contract_last(u...]
    all_gather x2 -> x0, waiting for transfers between devices: 150 us -> none  [the longest x1 80.9 us: per_device(): lax.all_gather(tokens, 'col', axis=0, tiled=True)]
    all_gather x3 -> x0, blocking collectives: 42 us -> none  [the longest x1 15 us: per_device(): lax.all_gather(gate_share, 'row', axis=0, tiled=True)]
    ppermute x0 -> x29, starting transfers between devices: none -> 40.4 us  [the longest x9 14.8 us: sum_over_row(): lax.ppermute(piece.astype(BF16), 'row', y_shift(k)).astype(F32)]
    ppermute x0 -> x29, waiting for transfers between devices: none -> 26.3 us  [the longest x6 11.2 us: gather_over_row(): got = lax.ppermute(share, 'row', y_shift(k))]
    all_to_all x0 -> x1, blocking collectives: none -> 20.1 us  [gather_z(): lax.all_to_all(copies, 'col', 0, 0, axis_index_groups=Z_GROUPS, tiled=True)]
    all_to_all x0 -> x2, starting transfers between devices: none -> 11.2 us  [the longest x1 7.8 us: per_device(): lax.all_to_all(pieces, 'col', 0, 0, axis_index_groups=Z_GROUPS, tiled=True)]
    all_to_all x0 -> x2, waiting for transfers between devices: none -> 10.6 us  [the longest x1 5.35 us: per_device(): lax.all_to_all(pieces, 'col', 0, 0, axis_index_groups=Z_GROUPS, tiled=True)]
  transfers between devices with their start and end apart: 4 -> 31, of which waited for: 4 -> 16; matrix products, arithmetic and copies ran while one was open for 5% -> 19% of each run, Pallas kernels for 0% -> 0%
where the time goes in v1:
time: 146 us; the launch traced here: 144 us
  starting transfers between devices  51.6 us (35%)
  waiting for transfers between devices  36.9 us (25%)
  blocking collectives  20.1 us (14%)
  matrix products  16.7 us (11%)
  local copies, waits for them, and re-layouts  9.6 us (7%)
  other arithmetic  8.25 us (6%)
    all_to_all x1, blocking collectives, gather_z(): lax.all_to_all(copies, 'col', 0, 0, axis_index_groups=Z_GROUPS, tiled=True)  20.1 us
    ppermute x9, starting transfers between devices, sum_over_row(): lax.ppermute(piece.astype(BF16), 'row', y_shift(k)).astype(F32)  14.8 us
    ppermute x6, waiting for transfers between devices, gather_over_row(): got = lax.ppermute(share, 'row', y_shift(k))  11.2 us
    ppermute x6, starting transfers between devices, gather_x(): lax.ppermute(plane, 'col', x_shift(k))  10.2 us
    ppermute x6, starting transfers between devices, gather_over_row(): got = lax.ppermute(share, 'row', y_shift(k))  9.23 us
    ppermute x3, waiting for transfers between devices, per_device(): lax.ppermute(planes[at].astype(BF16), 'col', x_shift(k)).astype(F32)  9.12 us
    dot_general x3, matrix products, contract_first(): lax.dot_general(left, right, (((0,), (0,)), ((), ())), preferred_element_...  8.76 us
    all_to_all x1, starting transfers between devices, per_device(): lax.all_to_all(pieces, 'col', 0, 0, axis_index_groups=Z_GROUPS, tiled=True)  7.8 us
  transfers between devices with their start and end apart: 31, of which 16 were waited for; matrix products, arithmetic and copies ran while one was open for 19% of the time, Pallas kernels for 0%

profile of v1, /device:TPU:8, one launch (start us, length us, event | category | flops | bytes accessed | tf_op | source)
XLA Modules:
  0.0 144.2 jit_solution(14590185298629659031)
XLA Ops:
  1.6 20.1 %all_to_all.15 = bf16[8,16,1024]{2,1,0:T(8,128)(2,1)S(1)} all-to-all(bf16[8,16,1024]{2,1,0:T(8,128)(2,1)S(1)} %broadcast_in_dim.20), channel_id=1, replica_groups={{0,1,2,3,4,5,6,7},{8,9,10,11,12,13,14,15},{16,17,18,19,20,21,22,23},{24..., dimensions={0} | all-to-all | bytes 524288 | tf_op jit(solution)/shard_map/all_to_all | solution.py:32
  23.2 3.4 %all-to-all-start = ((bf16[8,16,1024]{2,1,0:T(8,128)(2,1)}), bf16[8,16,1024]{2,1,0:T(8,128)(2,1)S(1)}, u32[]{:S(2)}, u32[]{:S(2)}) async-start(bf16[8,16,1024]{2,1,0:T(8,128)(2,1)} %broadcast_in_dim.9), calls=%async_computation | async-start | bytes 524288 | tf_op jit(solution)/shard_map/all_to_all | solution.py:32
  26.6 3.1 %collective-permute-start.9 = (bf16[128,1024]{1,0:T(8,128)(2,1)S(1)}, bf16[128,1024]{1,0:T(8,128)(2,1)S(1)}, u32[]{:S(2)}, u32[]{:S(2)}) collective-permute-start(bf16[128,1024]{1,0:T(8,128)(2,1)S(1)} %bitcast.8), channel_id=1, source_target_pairs={{0,16},{1,17},{2,18},{3,19},{4,20},{5,21},{6,22},{7,23},{8,24},{9,... | collective-permute-start | bytes 786440 | tf_op jit(solution)/shard_map/ppermute | solution.py:37
  31.7 5.3 %all-to-all-done = bf16[8,16,1024]{2,1,0:T(8,128)(2,1)S(1)} async-done(((bf16[8,16,1024]{2,1,0:T(8,128)(2,1)}), bf16[8,16,1024]{2,1,0:T(8,128)(2,1)S(1)}, u32[]{:S(2)}, u32[]{:S(2)}) %all-to-all-start) | async-done | bytes 262176 | tf_op jit(solution)/shard_map/all_to_all | solution.py:32
  37.0 3.0 %collective-permute-start.2 = (bf16[128,1024]{1,0:T(8,128)(2,1)S(1)}, bf16[128,1024]{1,0:T(8,128)(2,1)S(1)}, u32[]{:S(2)}, u32[]{:S(2)}) collective-permute-start(bf16[128,1024]{1,0:T(8,128)(2,1)S(1)} %bitcast.15), channel_id=1, source_target_pairs={{0,16},{1,17},{2,18},{3,19},{4,20},{5,21},{6,22},{7,23},{8,24},{9,... | collective-permute-start | bytes 786440 | tf_op jit(solution)/shard_map/ppermute | solution.py:37
  45.4 2.8 %fusion.19 = f32[512,896]{1,0:T(8,128)S(1)} fusion(bf16[1024,896]{1,0:T(8,128)(2,1)} %param.8, bf16[128,1024]{1,0:T(8,128)(2,1)S(1)} %collective-permute-done.9, bf16[128,1024]{1,0:T(8,128)(2,1)S(1)} %collective-permute-done.8, bf16[128,1024]{1,0:T(8,128)(2,1)S(1)} %collective-permute-done.7, bf16[128,1024]{1,0:T(8,128)(2,1)S(1)} %bitcast.11), kind=kOutput, calls=%fused_computation.59 | convolution fusion | flops 943718400 | bytes 4718592 | tf_op jit(solution)/shard_map/dot_general | solution.py:51
  60.6 3.5 %collective-permute-start.11 = (bf16[64,896]{1,0:T(8,128)(2,1)S(1)}, bf16[64,896]{1,0:T(8,128)(2,1)S(1)}, u32[]{:S(2)}, u32[]{:S(2)}) collective-permute-start(bf16[64,896]{1,0:T(8,128)(2,1)S(1)} %get-tuple-element.18), channel_id=1, source_target_pairs={{0,128},{32,160},{64,192},{96,224},{128,0},{160,32},{192,64},{224,... | collective-permute-start | bytes 344072 | tf_op jit(solution)/shard_map/ppermute | solution.py:61
  65.8 1.9 %collective-permute-start.16 = (bf16[64,896]{1,0:T(8,128)(2,1)S(1)}, bf16[64,896]{1,0:T(8,128)(2,1)S(1)}, u32[]{:S(2)}, u32[]{:S(2)}) collective-permute-start(bf16[64,896]{1,0:T(8,128)(2,1)S(1)} %get-tuple-element.17), channel_id=1, source_target_pairs={{0,64},{32,96},{64,128},{96,160},{128,192},{160,224},{192,0},{224,... | collective-permute-start | bytes 344072 | tf_op jit(solution)/shard_map/ppermute | solution.py:61
  69.2 2.0 %collective-permute-start.6 = (bf16[64,896]{1,0:T(8,128)(2,1)S(1)}, bf16[64,896]{1,0:T(8,128)(2,1)S(1)}, u32[]{:S(2)}, u32[]{:S(2)}) collective-permute-start(bf16[64,896]{1,0:T(8,128)(2,1)S(1)} %get-tuple-element.13), channel_id=1, source_target_pairs={{0,192},{32,224},{64,0},{96,32},{128,64},{160,96},{192,128},{224,1... | collective-permute-start | bytes 344072 | tf_op jit(solution)/shard_map/ppermute | solution.py:61
  71.3 3.5 %collective-permute-start.4 = (bf16[64,896]{1,0:T(8,128)(2,1)S(1)}, bf16[64,896]{1,0:T(8,128)(2,1)S(1)}, u32[]{:S(2)}, u32[]{:S(2)}) collective-permute-start(bf16[64,896]{1,0:T(8,128)(2,1)S(1)} %get-tuple-element.12), channel_id=1, source_target_pairs={{0,128},{32,160},{64,192},{96,224},{128,0},{160,32},{192,64},{224,... | collective-permute-start | bytes 344072 | tf_op jit(solution)/shard_map/ppermute | solution.py:61
  79.2 2.9 %collective-permute-start.18 = (bf16[64,1792]{1,0:T(8,128)(2,1)}, bf16[64,1792]{1,0:T(8,128)(2,1)}, u32[]{:S(2)}, u32[]{:S(2)}) collective-permute-start(bf16[64,1792]{1,0:T(8,128)(2,1)} %get-tuple-element.21), channel_id=1, source_target_pairs={{0,128},{32,160},{64,192},{96,224},{128,0},{160,32},{192,64},{224,... | collective-permute-start | bytes 688136 | tf_op jit(solution)/shard_map/ppermute | solution.py:75
  84.1 5.0 %collective-permute-done.18 = bf16[64,1792]{1,0:T(8,128)(2,1)} collective-permute-done((bf16[64,1792]{1,0:T(8,128)(2,1)}, bf16[64,1792]{1,0:T(8,128)(2,1)}, u32[]{:S(2)}, u32[]{:S(2)}) %collective-permute-start.18) | collective-permute-done | bytes 229408 | tf_op jit(solution)/shard_map/ppermute | solution.py:75
  90.0 1.8 %collective-permute-done.19 = bf16[64,1792]{1,0:T(8,128)(2,1)S(1)} collective-permute-done((bf16[64,1792]{1,0:T(8,128)(2,1)}, bf16[64,1792]{1,0:T(8,128)(2,1)S(1)}, u32[]{:S(2)}, u32[]{:S(2)}) %collective-permute-start.19) | collective-permute-done | bytes 229408 | tf_op jit(solution)/shard_map/ppermute | solution.py:75
  92.0 2.3 %collective-permute-start.25 = (bf16[64,896]{1,0:T(8,128)(2,1)}, bf16[64,896]{1,0:T(8,128)(2,1)}, u32[]{:S(2)}, u32[]{:S(2)}) collective-permute-start(bf16[64,896]{1,0:T(8,128)(2,1)} %get-tuple-element.5), channel_id=1, source_target_pairs={{0,128},{32,160},{64,192},{96,224},{128,0},{160,32},{192,64},{224,... | collective-permute-start | bytes 344072 | tf_op jit(solution)/shard_map/ppermute | solution.py:75
  96.3 3.5 %collective-permute-done.25 = bf16[64,896]{1,0:T(8,128)(2,1)} collective-permute-done((bf16[64,896]{1,0:T(8,128)(2,1)}, bf16[64,896]{1,0:T(8,128)(2,1)}, u32[]{:S(2)}, u32[]{:S(2)}) %collective-permute-start.25) | collective-permute-done | bytes 114720 | tf_op jit(solution)/shard_map/ppermute | solution.py:75
  101.9 1.9 %maximum_select_fusion = bf16[512,1792]{1,0:T(8,128)(2,1)S(1)} fusion(bf16[256,1792]{1,0:T(8,128)(2,1)} %collective-permute-done.21, bf16[256,1792]{1,0:T(8,128)(2,1)S(1)} %constant_dynamic-update-slice_fusion.4, pred[]{:T(512)S(6)} %eq.21), kind=kLoop, calls=%fused_computation | loop fusion | flops 8257536 | bytes 3670017 | tf_op jit(solution)/shard_map/jit(_where)/select_n | solution.py:78
  107.6 2.4 %collective-permute-start.23 = (bf16[128,1024]{1,0:T(8,128)(2,1)S(1)}, bf16[128,1024]{1,0:T(8,128)(2,1)S(1)}, u32[]{:S(2)}, u32[]{:S(2)}) collective-permute-start(bf16[128,1024]{1,0:T(8,128)(2,1)S(1)} %get-tuple-element.11), channel_id=1, source_target_pairs={{0,24},{1,25},{2,26},{3,27},{4,28},{5,29},{6,30},{7,31},{8,0},{9,1... | collective-permute-start | bytes 786440 | tf_op jit(solution)/shard_map/ppermute | solution.py:90
  111.6 2.4 %convolution_convert_fusion = bf16[896,1024]{1,0:T(8,128)(2,1)} fusion(bf16[256,896]{1,0:T(8,128)(2,1)S(1)} %collective-permute-done.28, bf16[256,896]{1,0:T(8,128)(2,1)S(1)} %constant_dynamic-update-slice_fusion, pred[]{:T(512)S(6)} %eq.21, bf16[128,1024]{1,0:T(8,128)(2,1)S(1)} %copy-done.19, bf16[128,1024]{1,0:T(8,128)(2,1)S(1)} %copy-done.21, ...), kind=kOutput, calls=%fused_computation.1 | convolution fusion | flops 948764672 | bytes 3801089 | tf_op jit(solution)/shard_map/dot_general | solution.py:23
  114.0 2.7 %collective-permute-done.24 = bf16[128,1024]{1,0:T(8,128)(2,1)S(1)} collective-permute-done((bf16[128,1024]{1,0:T(8,128)(2,1)S(1)}, bf16[128,1024]{1,0:T(8,128)(2,1)S(1)}, u32[]{:S(2)}, u32[]{:S(2)}) %collective-permute-start.24) | collective-permute-done | bytes 262176 | tf_op jit(solution)/shard_map/ppermute | solution.py:90
  116.7 4.9 %collective-permute-done.23 = bf16[128,1024]{1,0:T(8,128)(2,1)S(1)} collective-permute-done((bf16[128,1024]{1,0:T(8,128)(2,1)S(1)}, bf16[128,1024]{1,0:T(8,128)(2,1)S(1)}, u32[]{:S(2)}, u32[]{:S(2)}) %collective-permute-start.23) | collective-permute-done | bytes 262176 | tf_op jit(solution)/shard_map/ppermute | solution.py:90
  124.0 7.8 %all-to-all-start.2 = ((bf16[8,16,1024]{2,1,0:T(8,128)(2,1)}), bf16[8,16,1024]{2,1,0:T(8,128)(2,1)S(1)}, u32[]{:S(2)}, u32[]{:S(2)}) async-start(bf16[8,16,1024]{2,1,0:T(8,128)(2,1)} %bitcast.2), calls=%async_computation.2 | async-start | bytes 524288 | tf_op jit(solution)/shard_map/all_to_all | solution.py:92
  131.9 3.8 %convolution_convert_fusion.2 = bf16[1024,896]{1,0:T(8,128)(2,1)} fusion(bf16[512,1792]{1,0:T(8,128)(2,1)} %copy-done.1, bf16[128,1024]{1,0:T(8,128)(2,1)S(1)} %copy-done.13, bf16[128,1024]{1,0:T(8,128)(2,1)S(1)} %copy-done.15, bf16[128,1024]{1,0:T(8,128)(2,1)S(1)} %copy-done.17, bf16[128,1024]{1,0:T(8,128)(2,1)S(1)} %bitcast.13), kind=kOutput, calls=%fused_computation.3 | convolution fusion | flops 944635904 | bytes 3801088 | tf_op jit(solution)/shard_map/dot_general | solution.py:23
  135.7 2.5 %convolution_convert_fusion.1 = bf16[1024,896]{1,0:T(8,128)(2,1)} fusion(bf16[512,1792]{1,0:T(8,128)(2,1)S(1)} %copy-done.2, bf16[128,1024]{1,0:T(8,128)(2,1)S(1)} %copy-done.13, bf16[128,1024]{1,0:T(8,128)(2,1)S(1)} %copy-done.15, bf16[128,1024]{1,0:T(8,128)(2,1)S(1)} %copy-done.17, bf16[128,1024]{1,0:T(8,128)(2,1)S(1)} %bitcast.14), kind=kOutput, calls=%fused_computation.2 | convolution fusion | flops 944635904 | bytes 3801088 | tf_op jit(solution)/shard_map/dot_general | solution.py:23
  138.2 5.3 %all-to-all-done.2 = bf16[8,16,1024]{2,1,0:T(8,128)(2,1)S(1)} async-done(((bf16[8,16,1024]{2,1,0:T(8,128)(2,1)}), bf16[8,16,1024]{2,1,0:T(8,128)(2,1)S(1)}, u32[]{:S(2)}, u32[]{:S(2)}) %all-to-all-start.2) | async-done | bytes 262176 | tf_op jit(solution)/shard_map/all_to_all | solution.py:92
  (121 shorter events, 45.1 us)
Async XLA Ops:
  23.2 13.8 %all-to-all-start = ((bf16[8,16,1024]{2,1,0:T(8,128)(2,1)}), bf16[8,16,1024]{2,1,0:T(8,128)(2,1)S(1)}, u32[]{:S(2)}, u32[]{:S(2)}) async-start(bf16[8,16,1024]{2,1,0:T(8,128)(2,1)} %broadcast_in_dim.9), calls=%async_computation | async-start | bytes 524288 | tf_op jit(solution)/shard_map/all_to_all | solution.py:32
  26.6 14.6 %collective-permute-start.9 = (bf16[128,1024]{1,0:T(8,128)(2,1)S(1)}, bf16[128,1024]{1,0:T(8,128)(2,1)S(1)}, u32[]{:S(2)}, u32[]{:S(2)}) collective-permute-start(bf16[128,1024]{1,0:T(8,128)(2,1)S(1)} %bitcast.8), channel_id=1, source_target_pairs={{0,16},{1,17},{2,18},{3,19},{4,20},{5,21},{6,22},{7,23},{8,24},{9,... | collective-permute-start | bytes 786440 | tf_op jit(solution)/shard_map/ppermute | solution.py:37
  29.7 14.0 %collective-permute-start.8 = (bf16[128,1024]{1,0:T(8,128)(2,1)S(1)}, bf16[128,1024]{1,0:T(8,128)(2,1)S(1)}, u32[]{:S(2)}, u32[]{:S(2)}) collective-permute-start(bf16[128,1024]{1,0:T(8,128)(2,1)S(1)} %bitcast.9), channel_id=1, source_target_pairs={{0,24},{1,25},{2,26},{3,27},{4,28},{5,29},{6,30},{7,31},{8,0},{9,1... | collective-permute-start | bytes 786440 | tf_op jit(solution)/shard_map/ppermute | solution.py:37
  30.9 14.6 %collective-permute-start.7 = (bf16[128,1024]{1,0:T(8,128)(2,1)S(1)}, bf16[128,1024]{1,0:T(8,128)(2,1)S(1)}, u32[]{:S(2)}, u32[]{:S(2)}) collective-permute-start(bf16[128,1024]{1,0:T(8,128)(2,1)S(1)} %bitcast.10), channel_id=1, source_target_pairs={{0,8},{1,9},{2,10},{3,11},{4,12},{5,13},{6,14},{7,15},{8,16},{9,17... | collective-permute-start | bytes 786440 | tf_op jit(solution)/shard_map/ppermute | solution.py:37
  37.0 15.7 %collective-permute-start.2 = (bf16[128,1024]{1,0:T(8,128)(2,1)S(1)}, bf16[128,1024]{1,0:T(8,128)(2,1)S(1)}, u32[]{:S(2)}, u32[]{:S(2)}) collective-permute-start(bf16[128,1024]{1,0:T(8,128)(2,1)S(1)} %bitcast.15), channel_id=1, source_target_pairs={{0,16},{1,17},{2,18},{3,19},{4,20},{5,21},{6,22},{7,23},{8,24},{9,... | collective-permute-start | bytes 786440 | tf_op jit(solution)/shard_map/ppermute | solution.py:37
  40.0 12.7 %collective-permute-start.1 = (bf16[128,1024]{1,0:T(8,128)(2,1)S(1)}, bf16[128,1024]{1,0:T(8,128)(2,1)S(1)}, u32[]{:S(2)}, u32[]{:S(2)}) collective-permute-start(bf16[128,1024]{1,0:T(8,128)(2,1)S(1)} %bitcast.16), channel_id=1, source_target_pairs={{0,24},{1,25},{2,26},{3,27},{4,28},{5,29},{6,30},{7,31},{8,0},{9,1... | collective-permute-start | bytes 786440 | tf_op jit(solution)/shard_map/ppermute | solution.py:37
  41.2 11.6 %collective-permute-start = (bf16[128,1024]{1,0:T(8,128)(2,1)S(1)}, bf16[128,1024]{1,0:T(8,128)(2,1)S(1)}, u32[]{:S(2)}, u32[]{:S(2)}) collective-permute-start(bf16[128,1024]{1,0:T(8,128)(2,1)S(1)} %bitcast.17), channel_id=1, source_target_pairs={{0,8},{1,9},{2,10},{3,11},{4,12},{5,13},{6,14},{7,15},{8,16},{9,17... | collective-permute-start | bytes 786440 | tf_op jit(solution)/shard_map/ppermute | solution.py:37
  52.2 11.9 %collective-permute-start.14 = (f32[256,896]{1,0:T(8,128)}, f32[256,896]{1,0:T(8,128)}, u32[]{:S(2)}, u32[]{:S(2)}) collective-permute-start(f32[256,896]{1,0:T(8,128)} %constant_dynamic-slice_fusion), channel_id=1, source_target_pairs={{0,32},{32,0},{64,96},{96,64},{128,160},{160,128},{192,224},{224,1... | collective-permute-start | bytes 2752520 | tf_op jit(solution)/shard_map/ppermute | solution.py:57
  56.3 9.5 %collective-permute-start.3 = (f32[256,896]{1,0:T(8,128)}, f32[256,896]{1,0:T(8,128)S(1)}, u32[]{:S(2)}, u32[]{:S(2)}) collective-permute-start(f32[256,896]{1,0:T(8,128)} %constant_dynamic-slice_fusion.2), channel_id=1, source_target_pairs={{0,32},{32,0},{64,96},{96,64},{128,160},{160,128},{192,224},{224,1... | collective-permute-start | bytes 2752520 | tf_op jit(solution)/shard_map/ppermute | solution.py:57
  58.5 9.3 %collective-permute-start.13 = (bf16[64,896]{1,0:T(8,128)(2,1)S(1)}, bf16[64,896]{1,0:T(8,128)(2,1)S(1)}, u32[]{:S(2)}, u32[]{:S(2)}) collective-permute-start(bf16[64,896]{1,0:T(8,128)(2,1)S(1)} %get-tuple-element.19), channel_id=1, source_target_pairs={{0,192},{32,224},{64,0},{96,32},{128,64},{160,96},{192,128},{224,1... | collective-permute-start | bytes 344072 | tf_op jit(solution)/shard_map/ppermute | solution.py:61
  59.0 10.2 %collective-permute-start.12 = (bf16[64,896]{1,0:T(8,128)(2,1)S(1)}, bf16[64,896]{1,0:T(8,128)(2,1)S(1)}, u32[]{:S(2)}, u32[]{:S(2)}) collective-permute-start(bf16[64,896]{1,0:T(8,128)(2,1)S(1)} %get-tuple-element.20), channel_id=1, source_target_pairs={{0,64},{32,96},{64,128},{96,160},{128,192},{160,224},{192,0},{224,... | collective-permute-start | bytes 344072 | tf_op jit(solution)/shard_map/ppermute | solution.py:61
  60.6 10.6 %collective-permute-start.11 = (bf16[64,896]{1,0:T(8,128)(2,1)S(1)}, bf16[64,896]{1,0:T(8,128)(2,1)S(1)}, u32[]{:S(2)}, u32[]{:S(2)}) collective-permute-start(bf16[64,896]{1,0:T(8,128)(2,1)S(1)} %get-tuple-element.18), channel_id=1, source_target_pairs={{0,128},{32,160},{64,192},{96,224},{128,0},{160,32},{192,64},{224,... | collective-permute-start | bytes 344072 | tf_op jit(solution)/shard_map/ppermute | solution.py:61
  65.8 9.0 %collective-permute-start.16 = (bf16[64,896]{1,0:T(8,128)(2,1)S(1)}, bf16[64,896]{1,0:T(8,128)(2,1)S(1)}, u32[]{:S(2)}, u32[]{:S(2)}) collective-permute-start(bf16[64,896]{1,0:T(8,128)(2,1)S(1)} %get-tuple-element.17), channel_id=1, source_target_pairs={{0,64},{32,96},{64,128},{96,160},{128,192},{160,224},{192,0},{224,... | collective-permute-start | bytes 344072 | tf_op jit(solution)/shard_map/ppermute | solution.py:61
  69.2 7.6 %collective-permute-start.6 = (bf16[64,896]{1,0:T(8,128)(2,1)S(1)}, bf16[64,896]{1,0:T(8,128)(2,1)S(1)}, u32[]{:S(2)}, u32[]{:S(2)}) collective-permute-start(bf16[64,896]{1,0:T(8,128)(2,1)S(1)} %get-tuple-element.13), channel_id=1, source_target_pairs={{0,192},{32,224},{64,0},{96,32},{128,64},{160,96},{192,128},{224,1... | collective-permute-start | bytes 344072 | tf_op jit(solution)/shard_map/ppermute | solution.py:61
  79.2 9.9 %collective-permute-start.18 = (bf16[64,1792]{1,0:T(8,128)(2,1)}, bf16[64,1792]{1,0:T(8,128)(2,1)}, u32[]{:S(2)}, u32[]{:S(2)}) collective-permute-start(bf16[64,1792]{1,0:T(8,128)(2,1)} %get-tuple-element.21), channel_id=1, source_target_pairs={{0,128},{32,160},{64,192},{96,224},{128,0},{160,32},{192,64},{224,... | collective-permute-start | bytes 688136 | tf_op jit(solution)/shard_map/ppermute | solution.py:75
  82.1 9.7 %collective-permute-start.19 = (bf16[64,1792]{1,0:T(8,128)(2,1)}, bf16[64,1792]{1,0:T(8,128)(2,1)S(1)}, u32[]{:S(2)}, u32[]{:S(2)}) collective-permute-start(bf16[64,1792]{1,0:T(8,128)(2,1)} %get-tuple-element.21), channel_id=1, source_target_pairs={{0,64},{32,96},{64,128},{96,160},{128,192},{160,224},{192,0},{224,... | collective-permute-start | bytes 688136 | tf_op jit(solution)/shard_map/ppermute | solution.py:75
  82.9 9.0 %collective-permute-start.20 = (bf16[64,1792]{1,0:T(8,128)(2,1)}, bf16[64,1792]{1,0:T(8,128)(2,1)S(1)}, u32[]{:S(2)}, u32[]{:S(2)}) collective-permute-start(bf16[64,1792]{1,0:T(8,128)(2,1)} %get-tuple-element.21), channel_id=1, source_target_pairs={{0,192},{32,224},{64,0},{96,32},{128,64},{160,96},{192,128},{224,1... | collective-permute-start | bytes 688136 | tf_op jit(solution)/shard_map/ppermute | solution.py:75
  91.9 10.0 %collective-permute-start.21 = (bf16[256,1792]{1,0:T(8,128)(2,1)S(1)}, bf16[256,1792]{1,0:T(8,128)(2,1)}, u32[]{:S(2)}, u32[]{:S(2)}) collective-permute-start(bf16[256,1792]{1,0:T(8,128)(2,1)S(1)} %constant_dynamic-update-slice_fusion.4), channel_id=1, source_target_pairs={{0,32},{32,0},{64,96},{96,64},{128,160},{160,128},{192,224},{224,1... | collective-permute-start | bytes 2752520 | tf_op jit(solution)/shard_map/ppermute | solution.py:77
  92.0 7.9 %collective-permute-start.25 = (bf16[64,896]{1,0:T(8,128)(2,1)}, bf16[64,896]{1,0:T(8,128)(2,1)}, u32[]{:S(2)}, u32[]{:S(2)}) collective-permute-start(bf16[64,896]{1,0:T(8,128)(2,1)} %get-tuple-element.5), channel_id=1, source_target_pairs={{0,128},{32,160},{64,192},{96,224},{128,0},{160,32},{192,64},{224,... | collective-permute-start | bytes 344072 | tf_op jit(solution)/shard_map/ppermute | solution.py:75
  101.8 9.8 %collective-permute-start.28 = (bf16[256,896]{1,0:T(8,128)(2,1)S(1)}, bf16[256,896]{1,0:T(8,128)(2,1)S(1)}, u32[]{:S(2)}, u32[]{:S(2)}) collective-permute-start(bf16[256,896]{1,0:T(8,128)(2,1)S(1)} %constant_dynamic-update-slice_fusion), channel_id=1, source_target_pairs={{0,32},{32,0},{64,96},{96,64},{128,160},{160,128},{192,224},{224,1... | collective-permute-start | bytes 1376264 | tf_op jit(solution)/shard_map/ppermute | solution.py:77
  106.5 10.2 %collective-permute-start.24 = (bf16[128,1024]{1,0:T(8,128)(2,1)S(1)}, bf16[128,1024]{1,0:T(8,128)(2,1)S(1)}, u32[]{:S(2)}, u32[]{:S(2)}) collective-permute-start(bf16[128,1024]{1,0:T(8,128)(2,1)S(1)} %get-tuple-element.10), channel_id=1, source_target_pairs={{0,8},{1,9},{2,10},{3,11},{4,12},{5,13},{6,14},{7,15},{8,16},{9,17... | collective-permute-start | bytes 786440 | tf_op jit(solution)/shard_map/ppermute | solution.py:90
  107.6 14.0 %collective-permute-start.23 = (bf16[128,1024]{1,0:T(8,128)(2,1)S(1)}, bf16[128,1024]{1,0:T(8,128)(2,1)S(1)}, u32[]{:S(2)}, u32[]{:S(2)}) collective-permute-start(bf16[128,1024]{1,0:T(8,128)(2,1)S(1)} %get-tuple-element.11), channel_id=1, source_target_pairs={{0,24},{1,25},{2,26},{3,27},{4,28},{5,29},{6,30},{7,31},{8,0},{9,1... | collective-permute-start | bytes 786440 | tf_op jit(solution)/shard_map/ppermute | solution.py:90
  110.0 13.1 %collective-permute-start.22 = (bf16[128,1024]{1,0:T(8,128)(2,1)S(1)}, bf16[128,1024]{1,0:T(8,128)(2,1)S(1)}, u32[]{:S(2)}, u32[]{:S(2)}) collective-permute-start(bf16[128,1024]{1,0:T(8,128)(2,1)S(1)} %get-tuple-element.9), channel_id=1, source_target_pairs={{0,16},{1,17},{2,18},{3,19},{4,20},{5,21},{6,22},{7,23},{8,24},{9,... | collective-permute-start | bytes 786440 | tf_op jit(solution)/shard_map/ppermute | solution.py:90
  124.0 19.6 %all-to-all-start.2 = ((bf16[8,16,1024]{2,1,0:T(8,128)(2,1)}), bf16[8,16,1024]{2,1,0:T(8,128)(2,1)S(1)}, u32[]{:S(2)}, u32[]{:S(2)}) async-start(bf16[8,16,1024]{2,1,0:T(8,128)(2,1)} %bitcast.2), calls=%async_computation.2 | async-start | bytes 524288 | tf_op jit(solution)/shard_map/all_to_all | solution.py:92
  (31 other events, 246.7 us)
